TPU v7x, 32 devices: a whole 2x2x4 slice. The times are simulated.
32 devices in a mesh: clip: 2 (over x), bank: 16 (over z, y, core).
Axes of the slice: x: 2, y: 2, z: 4, core: 2. Of those that a mesh axis runs over, the one named last changes fastest.
Arguments:
- queries: bfloat16 [2, 256, 1536], P('clip', 'bank'), may hold values from -120 to 120
- keys: bfloat16 [2, 2048, 1536], P('clip', 'bank'), may hold values from -6 to 6
- values: bfloat16 [2, 2048, 1536], P('clip', 'bank'), may hold values from -6 to 6
- grad_out: bfloat16 [2, 256, 1536], P('clip', 'bank'), may hold values from -6 to 6
- null_key: bfloat16 [1536], replicated, may hold values from -4 to 4
- null_value: bfloat16 [1536], replicated, may hold values from -4 to 4
- bank_counts: int32 [2], P('clip'), may hold values from 128 to 2048, as said below
- block_slot: int32 [2, 16], P('clip', 'bank'), may hold values from 0 to 15, each once within a row
Outputs:
- grad_queries: bfloat16 [2, 256, 1536], P('clip', 'bank')
- grad_keys: bfloat16 [2, 2048, 1536], P('clip', 'bank')
- grad_values: bfloat16 [2, 2048, 1536], P('clip', 'bank')
- grad_null_key: float32 [1536], replicated
- grad_null_value: float32 [1536], replicated
Inputs may be any that keep to these rules, and one draw needn't show every extreme that they name: `bank_counts`: a multiple of 128; exactly one group holds 2048 live tokens. `block_slot`: each row is a permutation of the device indices.
All inputs are finite; a program needn't handle non-finite values.
Results may differ from a plain program's by a relative error of at most 0.01155.
Values may be sent and summed in bfloat16 or wider, within the bound.
A program may use at most 64 MiB of HBM per device.

v0:
```python
import jax
import jax.numpy as jnp
from jax import lax
from jax.sharding import PartitionSpec as P

HEADS = 12
HD = 128


def split_heads(matrix):
    return matrix.reshape(matrix.shape[0], HEADS, HD).transpose(1, 0, 2)


def join_heads(stacked):
    return stacked.transpose(1, 0, 2).reshape(stacked.shape[1], HEADS * HD)


def on_device(queries, keys, values, grad_out, null_key, null_value, bank_counts, block_slot):
    score_scale = HD ** (-0.5)
    whole_q, whole_do = (
        lax.all_gather(queries[0], "bank", axis=0, tiled=True),
        lax.all_gather(grad_out[0], "bank", axis=0, tiled=True),
    )
    row_count = whole_q.shape[0]
    block_rows = keys.shape[1]
    own_rows = queries.shape[1]
    valid_keys = jnp.clip(bank_counts[0] - block_slot[0, 0] * block_rows, 0, block_rows)
    live_keys = jnp.arange(block_rows, dtype=jnp.int32) < valid_keys
    live_float = live_keys.astype(jnp.float32)
    q_heads = split_heads(whole_q)
    do_heads = split_heads(whole_do)
    k_heads = split_heads(keys[0])
    v_heads = split_heads(values[0])
    nk_heads = null_key.reshape(HEADS, HD)
    nv_heads = null_value.reshape(HEADS, HD)
    null_score = (
        jnp.einsum("hqd,hd->hq", q_heads, nk_heads, preferred_element_type=jnp.float32)
        * score_scale
    )
    null_dp = jnp.einsum("hqd,hd->hq", do_heads, nv_heads, preferred_element_type=jnp.float32)

    def block_scores(q_head, k_head):
        scores = jnp.dot(q_head, k_head.T, preferred_element_type=jnp.float32) * score_scale
        return jnp.where(live_keys[None, :], scores, -1e30)

    def first_pass(pieces):
        q_head, k_head = pieces
        scores = block_scores(q_head, k_head)
        peaks = jnp.max(scores, axis=1)
        sums = jnp.sum(jnp.exp(scores - peaks[:, None]) * live_float[None, :], axis=1)
        return (peaks, sums)

    local_peaks, local_sums = lax.map(first_pass, (q_heads, k_heads))
    peaks_all = lax.pmax(local_peaks, "bank")
    sums_all = lax.psum(local_sums * jnp.exp(local_peaks - peaks_all), "bank")
    row_top = jnp.maximum(peaks_all, null_score)
    log_total = row_top + jnp.log(
        sums_all * jnp.exp(peaks_all - row_top) + jnp.exp(null_score - row_top)
    )
    null_prob = jnp.exp(null_score - log_total)

    def second_pass(pieces):
        q_head, k_head, do_head, v_head, log_head = pieces
        probs = jnp.exp(block_scores(q_head, k_head) - log_head[:, None]) * live_float[None, :]
        dprobs = jnp.dot(do_head, v_head.T, preferred_element_type=jnp.float32)
        return (probs, dprobs, jnp.sum(probs * dprobs, axis=1))

    probs_all, dprobs_all, partial_delta = lax.map(
        second_pass, (q_heads, k_heads, do_heads, v_heads, log_total)
    )
    row_delta = lax.psum(partial_delta, "bank") + null_prob * null_dp

    def third_pass(pieces):
        probs, dprobs, q_head, do_head, delta_head = pieces
        dscore = (probs * (dprobs - delta_head[:, None])).astype(jnp.bfloat16)
        grad_k = (
            jnp.dot(dscore.T, q_head, preferred_element_type=jnp.float32) * score_scale
        ).astype(jnp.bfloat16)
        grad_v = jnp.dot(
            probs.astype(jnp.bfloat16).T, do_head, preferred_element_type=jnp.float32
        ).astype(jnp.bfloat16)
        return (dscore, grad_k, grad_v)

    dscores, grad_k, grad_v = lax.map(
        third_pass, (probs_all, dprobs_all, q_heads, do_heads, row_delta)
    )
    product = jnp.einsum("hqk,hkd->qhd", dscores, k_heads, preferred_element_type=jnp.float32)
    own_terms = lax.psum_scatter(
        product.reshape(row_count, HEADS * HD) * score_scale,
        "bank",
        scatter_dimension=0,
        tiled=True,
    )
    row_start = lax.axis_index("bank") * own_rows
    null_ds = null_prob * (null_dp - row_delta)
    own_ds = lax.dynamic_slice_in_dim(null_ds, row_start, own_rows, 1)
    own_prob = lax.dynamic_slice_in_dim(null_prob, row_start, own_rows, 1)
    own_q = lax.dynamic_slice_in_dim(q_heads, row_start, own_rows, 1).astype(jnp.float32)
    own_do = lax.dynamic_slice_in_dim(do_heads, row_start, own_rows, 1).astype(jnp.float32)
    null_term = (
        own_ds[:, :, None] * nk_heads.astype(jnp.float32)[:, None, :] * score_scale
    ).transpose(1, 0, 2)
    grad_q = (own_terms + null_term.reshape(own_rows, HEADS * HD)).astype(jnp.bfloat16)
    local_nk = jnp.sum(own_ds[:, :, None] * own_q, axis=1) * score_scale
    local_nv = jnp.sum(own_prob[:, :, None] * own_do, axis=1)
    grad_nk, grad_nv = lax.psum((local_nk.reshape(-1), local_nv.reshape(-1)), ("clip", "bank"))
    return (grad_q[None], join_heads(grad_k)[None], join_heads(grad_v)[None], grad_nk, grad_nv)


def solution(mesh):
    return jax.shard_map(
        on_device,
        mesh=mesh,
        in_specs=(
            P("clip", "bank", None),
            P("clip", "bank", None),
            P("clip", "bank", None),
            P("clip", "bank", None),
            P(),
            P(),
            P("clip"),
            P("clip", "bank"),
        ),
        out_specs=(
            P("clip", "bank", None),
            P("clip", "bank", None),
            P("clip", "bank", None),
            P(),
            P(),
        ),
        check_vma=False,
    )
```

profile of v0, /device:TPU:0, one launch (start us, length us, event | category | flops | bytes accessed | tf_op | source)
XLA Modules:
  0.0 431.0 jit_solution(5510000980406469901)
XLA Ops:
  7.3 25.7 %all-gather = bf16[1,256,1536]{2,1,0:T(8,128)(2,1)S(1)} all-gather(bf16[1,16,1536]{2,1,0:T(8,128)(2,1)} %param.14), channel_id=2, replica_groups=mesh['clip'=2,'bank'=16] {'bank'}, dimensions={1}, use_global_device_ids=true | all-gather | bytes 835584 | tf_op jit(solution)/shard_map/all_gather | solution.py:21
  35.8 5.1 %while.45 = (s32[]{:T(128)}, f32[12,256]{1,0:T(8,128)S(1)}, f32[12,256]{1,0:T(8,128)S(1)}, bf16[12,256,128]{2,1,0:T(8,128)(2,1)S(1)}, bf16[12,128,128]{2,1,0:T(8...) while((s32[]{:T(128)}, f32[12,256]{1,0:T(8,128)S(1)}, f32[12,256]{1,0:T(8,128)S(1)}, ...), condition=%wide.region_3.4_spmd.clone.clone, body=%wide.region_0.3_spmd.clone.clone.sunk | while | flops 8584962 | bytes 370401 | solution.py:53
  40.9 57.8 %pmax.7 = f32[12,256]{1,0:T(8,128)S(1)} all-reduce(f32[12,256]{1,0:T(8,128)S(1)} %get-tuple-element.151), channel_id=1, replica_groups=mesh['clip'=2,'bank'=16] {'bank'}, use_global_device_ids=true, to_apply=%region_4.5 | all-reduce | flops 3072 | bytes 24576 | tf_op jit(solution)/shard_map/pmax | solution.py:54
  98.8 57.6 %psum.28 = f32[12,256]{1,0:T(8,128)} all-reduce(f32[12,256]{1,0:T(8,128)S(1)} %exponential_multiply_fusion), channel_id=1, replica_groups=mesh['clip'=2,'bank'=16] {'bank'}, use_global_device_ids=true, to_apply=%region_5.6 | all-reduce | flops 3072 | bytes 24576 | tf_op jit(solution)/shard_map/psum | solution.py:55
  156.6 19.8 %all-gather.1 = bf16[1,256,1536]{2,1,0:T(8,128)(2,1)S(1)} all-gather(bf16[1,16,1536]{2,1,0:T(8,128)(2,1)S(1)} %copy-done.9), channel_id=3, replica_groups=mesh['clip'=2,'bank'=16] {'bank'}, dimensions={1}, use_global_device_ids=true | all-gather | bytes 835584 | tf_op jit(solution)/shard_map/all_gather | solution.py:22
  177.1 1.9 copy.45
  179.0 1.4 fusion.55
  181.0 63.4 %while.46 = (s32[]{:T(128)}, f32[12,256,128]{1,2,0:T(8,128)}, f32[12,256,128]{1,2,0:T(8,128)}, f32[12,256]{1,0:T(8,128)}, bf16[12,256,128]{2,1,0:T(8,128)(2,1)S(...) while((s32[]{:T(128)}, f32[12,256,128]{1,2,0:T(8,128)}, ...), condition=%wide.region_8.9_spmd.clone.clone, body=%wide.region_6.8_spmd.clone.clone.sunk | while | flops 16973824 | bytes 994049 | solution.py:68
  181.7 1.6 bitcast_dynamic-update-slice_fusion.4
  183.3 1.6 bitcast_dynamic-update-slice_fusion.5
  185.0 1.3 dynamic_update_slice.56
  187.0 1.6 bitcast_dynamic-update-slice_fusion.4
  188.6 1.6 bitcast_dynamic-update-slice_fusion.5
  190.3 1.3 dynamic_update_slice.56
  192.3 1.6 bitcast_dynamic-update-slice_fusion.4
  193.9 1.6 bitcast_dynamic-update-slice_fusion.5
  195.5 1.3 dynamic_update_slice.56
  197.6 1.6 bitcast_dynamic-update-slice_fusion.4
  199.2 1.6 bitcast_dynamic-update-slice_fusion.5
  200.8 1.3 dynamic_update_slice.56
  202.8 1.6 bitcast_dynamic-update-slice_fusion.4
  204.4 1.6 bitcast_dynamic-update-slice_fusion.5
  208.1 1.6 bitcast_dynamic-update-slice_fusion.4
  209.7 1.6 bitcast_dynamic-update-slice_fusion.5
  211.4 1.3 dynamic_update_slice.56
  213.4 1.6 bitcast_dynamic-update-slice_fusion.4
  215.0 1.6 bitcast_dynamic-update-slice_fusion.5
  216.7 1.3 dynamic_update_slice.56
  218.7 1.6 bitcast_dynamic-update-slice_fusion.4
  220.3 1.6 bitcast_dynamic-update-slice_fusion.5
  222.0 1.3 dynamic_update_slice.56
  224.0 1.6 bitcast_dynamic-update-slice_fusion.4
  225.6 1.6 bitcast_dynamic-update-slice_fusion.5
  227.3 1.3 dynamic_update_slice.56
  229.3 1.6 bitcast_dynamic-update-slice_fusion.4
  230.9 1.6 bitcast_dynamic-update-slice_fusion.5
  234.6 1.6 bitcast_dynamic-update-slice_fusion.4
  236.2 1.6 bitcast_dynamic-update-slice_fusion.5
  239.8 1.6 bitcast_dynamic-update-slice_fusion.4
  241.4 1.6 bitcast_dynamic-update-slice_fusion.5
  244.4 59.1 %psum.29 = f32[12,256]{1,0:T(8,128)S(1)} all-reduce(f32[12,256]{1,0:T(8,128)} %get-tuple-element.155), channel_id=1, replica_groups=mesh['clip'=2,'bank'=16] {'bank'}, use_global_device_ids=true, to_apply=%region_9.10 | all-reduce | flops 3072 | bytes 24576 | tf_op jit(solution)/shard_map/psum | solution.py:71
  303.8 1.4 multiply_add_fusion
  305.1 57.2 %while.44 = (s32[]{:T(128)}, bf16[12,256,128]{2,1,0:T(8,128)(2,1)}, bf16[12,128,128]{1,2,0:T(8,128)(2,1)}, bf16[12,128,128]{1,2,0:T(8,128)(2,1)}, f32[12,256,128...) while((s32[]{:T(128)}, bf16[12,256,128]{2,1,0:T(8,128)(2,1)}, ...), condition=%wide.region_11.12_spmd, body=%wide.region_10.11_spmd.sunk | while | flops 16957440 | bytes 2101369 | solution.py:84
  362.3 1.6 convolution_multiply_fusion.3
  363.9 1.6 copy.54
  369.2 37.2 %all-reduce = (f32[1536]{0:T(1024)}, f32[1536]{0:T(1024)}) all-reduce(f32[1536]{0:T(1024)S(1)} %multiply_bitcast_fusion, f32[1536]{0:T(1024)S(1)} %bitcast.208), channel_id=1, replica_groups=mesh['clip'=2,'bank'=16] {'clip','bank'}, use_global_device_ids=true, to_apply=%region_14.15 | all-reduce | flops 3072 | bytes 24576 | tf_op jit(solution)/shard_map/psum | solution.py:106
  406.4 16.1 %reduce-scatter.2.cloned.1.call-done = f32[16,1536]{1,0:T(8,128)} async-done(((f32[256,1536]{1,0:T(8,128)}), f32[16,1536]{1,0:T(8,128)}) %reduce-scatter.2.cloned.1.call-update) | async-done | bytes 98320 | tf_op jit(solution)/shard_map/reduce_scatter | solution.py:88
  422.6 1.6 fusion.48
  (286 shorter events, 82.5 us)
Async XLA Ops:
  7.2 296.4 %copy-start = (bf16[1536]{0:T(1024)(128)(2,1)S(1)}, bf16[1536]{0:T(1024)(128)(2,1)}, u32[]{:S(2)}) copy-start(bf16[1536]{0:T(1024)(128)(2,1)} %param.19) | copy-start | bytes 9220
  7.2 415.3 %reduce-scatter.2.cloned.1.call-start = ((), (), s32[]{:S(2)}) async-start(), calls=%async_computation.1 | async-start | bytes 1671168 | tf_op jit(solution)/shard_map/reduce_scatter | solution.py:88
  33.0 1.0 copy-start.3
  34.2 146.8 %copy-start.1 = (bf16[1,128,1536]{1,2,0:T(8,128)(2,1)}, bf16[1,128,1536]{1,2,0:T(8,128)(2,1)S(1)}, u32[]{:S(2)}) copy-start(bf16[1,128,1536]{1,2,0:T(8,128)(2,1)S(1)} %copy.41) | copy-start | bytes 1179652
  34.2 122.1 %copy-start.11 = (bf16[1536]{0:T(1024)(128)(2,1)S(1)}, bf16[1536]{0:T(1024)(128)(2,1)}, u32[]{:S(2)}) copy-start(bf16[1536]{0:T(1024)(128)(2,1)} %param.18) | copy-start | bytes 9220
  34.5 122.1 %copy-start.9 = (bf16[1,16,1536]{2,1,0:T(8,128)(2,1)S(1)}, bf16[1,16,1536]{2,1,0:T(8,128)(2,1)}, u32[]{:S(2)}) copy-start(bf16[1,16,1536]{2,1,0:T(8,128)(2,1)} %param.17) | copy-start | bytes 147460
  40.9 115.7 %copy-start.2 = (bf16[12,128,128]{2,1,0:T(8,128)(2,1)}, bf16[12,128,128]{2,1,0:T(8,128)(2,1)S(1)}, u32[]{:S(2)}) copy-start(bf16[12,128,128]{2,1,0:T(8,128)(2,1)S(1)} %get-tuple-element.665) | copy-start | bytes 1179652
  98.7 57.9 %copy-start.6 = (f32[12,256]{1,0:T(8,128)}, f32[12,256]{1,0:T(8,128)S(1)}, u32[]{:S(2)}) copy-start(f32[12,256]{1,0:T(8,128)S(1)} %pmax.7) | copy-start | bytes 36868
  156.6 22.4 %copy-start.7 = (f32[12,1,256]{2,1,0:T(1,128)}, f32[12,1,256]{2,1,0:T(1,128)S(1)}, u32[]{:S(2)}) copy-start(f32[12,1,256]{2,1,0:T(1,128)S(1)} %fusion.63) | copy-start | bytes 36868
  365.5 0.7 copy-start.12
  365.5 0.7 copy-start.8
  365.5 0.7 copy-start.10
  365.5 1.0 copy-start.4
  365.5 2.0 copy-start.5
Sparse Core Ops, SparseCore 0:
  365.7 56.8 reduce-scatter.1
where the time goes:
time: 435 us; the launch traced here: 431 us
  blocking collectives  257 us (59%)
  local copies, waits for them, and re-layouts  77.6 us (18%)
  matrix products  47.8 us (11%)
  waiting for transfers between devices  16.1 us (4%)
  other arithmetic  15.8 us (4%)
  between operations  15.6 us (4%)
    psum x1, blocking collectives, on_device(): row_delta = lax.psum(partial_delta, 'bank') + null_prob * null_dp  59.1 us
    pmax x1, blocking collectives, on_device(): peaks_all = lax.pmax(local_peaks, 'bank')  57.8 us
    psum x1, blocking collectives, on_device(): sums_all = lax.psum(local_sums * jnp.exp(local_peaks - peaks_all), 'bank')  57.6 us
    psum x1, blocking collectives, on_device(): lax.psum((local_nk.reshape(-1), local_nv.reshape(-1)), ('clip', 'bank'))  37.2 us
    all_gather x1, blocking collectives, on_device(): lax.all_gather(queries[0], 'bank', axis=0, tiled=True)  25.7 us
    dynamic_slice x48, local copies, waits for them, and re-layouts, on_device(): lax.map(third_pass, (probs_all, dprobs_all, q_heads, do_heads, row_delta))  24.1 us
    dot_general x24, matrix products, block_scores(): jnp.dot(q_head, k_head.T, preferred_element_type=jnp.float32) * score_scale  21.5 us
    all_gather x1, blocking collectives, on_device(): lax.all_gather(grad_out[0], 'bank', axis=0, tiled=True)  19.8 us
  transfers between devices with their start and end apart: 1, of which 1 were waited for; matrix products, arithmetic and copies ran while one was open for 1% of the time, Pallas kernels for 0%

commit v1 on v0

v1 whole, which is shorter than its diff:
```python
import functools

import jax
import jax.numpy as jnp
from jax import lax
from jax.experimental import pallas as pl
from jax.experimental.pallas import tpu as pltpu
from jax.sharding import PartitionSpec as P

HEADS = 12
HD = 128
HW = HEADS * HD
SCALE = HD ** (-0.5)
F32 = jnp.float32
BF16 = jnp.bfloat16
NT = (((1,), (1,)), ((), ()))
TN = (((0,), (0,)), ((), ()))


def nt_dot(a, b):
    return lax.dot_general(a, b, NT, preferred_element_type=F32)


def halves(x):
    high = x.astype(BF16)
    return high, (x - high.astype(F32)).astype(BF16)


def merge(lses, deltas):
    top = functools.reduce(jnp.maximum, lses)
    weights = [jnp.exp(one - top) for one in lses]
    total = sum(weights[1:], weights[0])
    mixed = weights[0] * deltas[0]
    for weight, delta in zip(weights[1:], deltas[1:]):
        mixed = mixed + weight * delta
    return top + jnp.log(total), mixed / total


def kernel(
    n_clip, n_z, rows, blk,
    valid_ref, q_ref, k_ref, v_ref, do_ref, nk_ref, nv_ref,
    gq_ref, gk_ref, gv_ref, gnk_ref, gnv_ref,
    q_all, do_all, e_s, dp_s, p_s, ds_s, dq_s, dq_out, rs_c, y_out, rs_y, acc_s, z_out, rs_z,
    peak_s, st_lo, st_z, null_s, null_sums,
    g_recv, g_send_z, g_send_y, g_send_c, st_send, st_recv, rs_send, rs_recv, n_send, n_recv,
):
    n = 4 * n_z
    qt = n * rows
    clip = lax.axis_index("clip")
    bank = lax.axis_index("bank")
    core = lax.rem(bank, 2)
    y = lax.rem(bank // 2, 2)
    z = bank // 4

    def dev(z_, y_, c_):
        return (clip, (z_ * 2 + y_) * 2 + c_)

    def place(z_, y_, c_):
        return (c_ * 2 + y_) * n_z + z_

    mine = place(z, y, core)
    others_z = [lax.rem(z + j, n_z) for j in range(1, n_z)]
    lo_peers = [(y, 1 - core), (1 - y, core), (1 - y, 1 - core)]
    to_core, to_y = dev(z, y, 1 - core), dev(z, 1 - y, core)
    clip_peers = [lax.rem(clip + j, n_clip) for j in range(1, n_clip)]

    barrier = pltpu.get_barrier_semaphore()
    peers = [dev(z, a, b) for a, b in lo_peers] + [dev(o, y, core) for o in others_z]
    peers += [(o, bank) for o in clip_peers]
    for peer in peers:
        pl.semaphore_signal(barrier, inc=1, device_id=peer, device_id_type=pl.DeviceIdType.MESH)
    pl.semaphore_wait(barrier, len(peers))

    def remote(src, dst, send, recv, device):
        copy = pltpu.make_async_remote_copy(
            src_ref=src, dst_ref=dst, send_sem=send, recv_sem=recv,
            device_id=device, device_id_type=pl.DeviceIdType.MESH,
        )
        copy.start()
        return copy

    gathered = ((q_ref, q_all), (do_ref, do_all))
    sends = []

    def own_sends(a):
        src, dst = gathered[a]
        for j, o in enumerate(others_z):
            sends.append(remote(src, dst.at[mine], g_send_z.at[a, j], g_recv.at[a, mine], dev(o, y, core)))
        sends.append(remote(src, dst.at[mine], g_send_y.at[a, 0], g_recv.at[a, mine], to_y))
        sends.append(remote(src, dst.at[mine], g_send_c.at[a, 0], g_recv.at[a, mine], to_core))

    def arrived(a, at):
        dst = gathered[a][1]
        pltpu.make_async_remote_copy(
            src_ref=dst.at[at], dst_ref=dst.at[at], send_sem=g_send_z.at[a, 0], recv_sem=g_recv.at[a, at],
            device_id=to_core, device_id_type=pl.DeviceIdType.MESH,
        ).wait_recv()

    def pass_on(a, at, send, to):
        dst = gathered[a][1]
        sends.append(remote(dst.at[at], dst.at[at], send, g_recv.at[a, at], to))

    def forward(a):
        for j, o in enumerate(others_z):
            at = place(o, y, core)
            arrived(a, at)
            pass_on(a, at, g_send_y.at[a, j + 1], to_y)
            pass_on(a, at, g_send_c.at[a, j + 1], to_core)
        for j, o in enumerate([z] + others_z):
            at = place(o, 1 - y, core)
            arrived(a, at)
            pass_on(a, at, g_send_c.at[a, n_z + j], to_core)

    def from_core(a):
        for o in [z] + others_z:
            arrived(a, place(o, y, 1 - core))
        for o in [z] + others_z:
            arrived(a, place(o, 1 - y, 1 - core))

    own_sends(0)
    own_sends(1)
    q_all[mine] = q_ref[...]
    do_all[mine] = do_ref[...]
    forward(0)
    from_core(0)
    forward(1)

    live = lax.broadcasted_iota(jnp.int32, (blk, qt), 0) < valid_ref[0, 0]
    lo = core * 2 + y

    def cols(h):
        return slice(h * HD, (h + 1) * HD)

    def head_of(ref, h):
        return ref[:, :, cols(h)].reshape(qt, HD)

    totals = []
    for h in range(HEADS):
        scores = nt_dot(k_ref[:, cols(h)], head_of(q_all, h)) * SCALE
        scores = jnp.where(live, scores, -1e30)
        peak = jnp.max(scores, axis=0, keepdims=True)
        e = jnp.exp(scores - peak)
        total = jnp.sum(e, axis=0, keepdims=True)
        e_s[h] = e
        peak_s[h : h + 1, :] = peak
        st_lo[lo, h : h + 1, :] = peak + jnp.log(total)
        totals.append(total)
    from_core(1)
    for h in range(HEADS):
        dp = nt_dot(v_ref[:, cols(h)], head_of(do_all, h))
        dp_s[h] = dp
        st_lo[lo, HEADS + h : HEADS + h + 1, :] = jnp.sum(e_s[h] * dp, axis=0, keepdims=True) / totals[h]

    st = [
        remote(st_lo.at[lo], st_lo.at[lo], st_send.at[0, i], st_recv.at[0, lo], dev(z, a, b))
        for i, (a, b) in enumerate(lo_peers)
    ]
    row_of = lax.broadcasted_iota(jnp.int32, (16, HW), 0)
    col_of = lax.broadcasted_iota(jnp.int32, (16, HW), 1)
    diagonal = (col_of >= row_of * HD) & (col_of < (row_of + 1) * HD)
    nk_diag = jnp.where(diagonal, jnp.broadcast_to(nk_ref[...].astype(F32), (16, HW)), 0.0).astype(BF16)
    nv_diag = jnp.where(diagonal, jnp.broadcast_to(nv_ref[...].astype(F32), (16, HW)), 0.0).astype(BF16)
    whole_q = q_all[...].reshape(qt, HW)
    whole_do = do_all[...].reshape(qt, HW)
    null_score = (nt_dot(nk_diag, whole_q) * SCALE)[:HEADS]
    null_dp = nt_dot(nv_diag, whole_do)[:HEADS]

    def stat_arrived(stage, buf, at):
        pltpu.make_async_remote_copy(
            src_ref=buf.at[at], dst_ref=buf.at[at], send_sem=st_send.at[stage, 0], recv_sem=st_recv.at[stage, at],
            device_id=to_core, device_id_type=pl.DeviceIdType.MESH,
        ).wait_recv()

    for a, b in lo_peers:
        stat_arrived(0, st_lo, b * 2 + a)
    lse, delta = merge([st_lo[i, :HEADS] for i in range(4)], [st_lo[i, HEADS:] for i in range(4)])
    st_z[z, :HEADS, :] = lse
    st_z[z, HEADS:, :] = delta
    for j, o in enumerate(others_z):
        st.append(remote(st_z.at[z], st_z.at[z], st_send.at[1, j], st_recv.at[1, z], dev(o, y, core)))
    for o in others_z:
        stat_arrived(1, st_z, o)
    lse, delta = merge([st_z[i, :HEADS] for i in range(n_z)], [st_z[i, HEADS:] for i in range(n_z)])
    top = jnp.maximum(lse, null_score)
    log_total = top + jnp.log(jnp.exp(lse - top) + jnp.exp(null_score - top))
    null_prob = jnp.exp(null_score - log_total)
    delta = jnp.exp(lse - log_total) * delta + null_prob * null_dp
    null_ds = null_prob * (null_dp - delta)
    factor = jnp.exp(peak_s[:HEADS] - log_total)

    for h in range(HEADS):
        probs = e_s[h] * factor[h : h + 1]
        dscore = (probs * (dp_s[h] - delta[h : h + 1])).astype(BF16)
        p_s[h] = probs.astype(BF16)
        ds_s[h] = dscore
        dq = lax.dot_general(dscore, k_ref[:, cols(h)], TN, preferred_element_type=F32) * SCALE
        dq = dq.reshape(2, 2 * n_z, rows, HD)
        dq_s[:, :, :, cols(h)] = dq
        dq_out[:, :, :, cols(h)] = dq.astype(BF16)

    rs = [remote(dq_out.at[1 - core], rs_c, rs_send.at[0], rs_recv.at[0], to_core)]

    null_s[0, :HEADS, :] = null_ds
    null_s[1, :HEADS, :] = null_prob
    null_s[:, HEADS:, :] = jnp.zeros((2, 16 - HEADS, qt), F32)
    ds_high, ds_low = halves(null_s[0])
    p_high, p_low = halves(null_s[1])

    def dot(a, b):
        return jnp.dot(a, b, preferred_element_type=F32)

    sum_k = jnp.where(diagonal, dot(ds_high, whole_q) + dot(ds_low, whole_q), 0.0) * SCALE
    sum_v = jnp.where(diagonal, dot(p_high, whole_do) + dot(p_low, whole_do), 0.0)
    null_sums[clip, 0:1, :] = jnp.sum(sum_k, axis=0, keepdims=True)
    null_sums[clip, 1:2, :] = jnp.sum(sum_v, axis=0, keepdims=True)
    ns = [
        remote(null_sums.at[clip], null_sums.at[clip], n_send.at[j], n_recv.at[clip], (o, bank))
        for j, o in enumerate(clip_peers)
    ]

    own_at = lax.broadcasted_iota(jnp.int32, (rows, qt), 1) - mine * rows
    pick = (own_at == lax.broadcasted_iota(jnp.int32, (rows, qt), 0)).astype(F32).astype(BF16)
    own_high = nt_dot(pick, ds_high).astype(BF16)
    own_low = nt_dot(pick, ds_low).astype(BF16)
    null_term = (dot(own_high, nk_diag) + dot(own_low, nk_diag)) * SCALE

    rs[0].wait_recv()
    far = pl.ds((1 - y) * n_z, n_z)
    near = pl.ds(y * n_z, n_z)
    y_out[...] = (dq_s[core, far] + rs_c[far].astype(F32)).astype(BF16)
    rs.append(remote(y_out, rs_y, rs_send.at[1], rs_recv.at[1], to_y))
    acc_s[...] = dq_s[core, near] + rs_c[near].astype(F32)
    for h in range(HEADS):
        gv_ref[:, cols(h)] = dot(p_s[h], head_of(do_all, h)).astype(BF16)
    rs[1].wait_recv()
    acc = acc_s[...] + rs_y[...].astype(F32)
    acc_s[...] = acc
    z_out[...] = acc.astype(BF16)
    for j, o in enumerate(others_z):
        rs.append(remote(z_out.at[o], rs_z.at[z], rs_send.at[2 + j], rs_recv.at[2 + z], dev(o, y, core)))
    for h in range(HEADS):
        gk_ref[:, cols(h)] = (dot(ds_s[h], head_of(q_all, h)) * SCALE).astype(BF16)
    total = acc_s[z] + null_term
    for o in others_z:
        pltpu.make_async_remote_copy(
            src_ref=z_out.at[o], dst_ref=rs_z.at[o], send_sem=rs_send.at[2], recv_sem=rs_recv.at[2 + o],
            device_id=to_core, device_id_type=pl.DeviceIdType.MESH,
        ).wait_recv()
        total = total + rs_z[o].astype(F32)
    gq_ref[...] = total.astype(BF16)
    for o in clip_peers:
        pltpu.make_async_remote_copy(
            src_ref=null_sums.at[o], dst_ref=null_sums.at[o], send_sem=n_send.at[0], recv_sem=n_recv.at[o],
            device_id=to_core, device_id_type=pl.DeviceIdType.MESH,
        ).wait_recv()
    both = null_sums[0]
    for i in range(1, n_clip):
        both = both + null_sums[i]
    gnk_ref[...] = both[0:1]
    gnv_ref[...] = both[1:2]
    for copy in sends + st + rs + ns:
        copy.wait_send()


def on_device(n_clip, n_bank, queries, keys, values, grad_out, null_key, null_value, bank_counts, block_slot):
    own_rows = queries.shape[1]
    rows = -(-own_rows // 16) * 16
    blk = keys.shape[1]
    q, do = queries[0], grad_out[0]
    if rows != own_rows:
        q = jnp.pad(q, ((0, rows - own_rows), (0, 0)))
        do = jnp.pad(do, ((0, rows - own_rows), (0, 0)))
    n_z = n_bank // 4
    qt = n_bank * rows
    valid = jnp.clip(bank_counts[0] - block_slot * blk, 0, blk)
    vmem = pl.BlockSpec(memory_space=pltpu.VMEM)
    dma = pltpu.SemaphoreType.DMA
    gq, gk, gv, gnk, gnv = pl.pallas_call(
        functools.partial(kernel, n_clip, n_z, rows, blk),
        out_shape=(
            jax.ShapeDtypeStruct((rows, HW), BF16),
            jax.ShapeDtypeStruct((blk, HW), BF16),
            jax.ShapeDtypeStruct((blk, HW), BF16),
            jax.ShapeDtypeStruct((1, HW), F32),
            jax.ShapeDtypeStruct((1, HW), F32),
        ),
        in_specs=[pl.BlockSpec(memory_space=pltpu.SMEM)] + [vmem] * 6,
        out_specs=[vmem] * 5,
        scratch_shapes=[
            pltpu.VMEM((n_bank, rows, HW), BF16),
            pltpu.VMEM((n_bank, rows, HW), BF16),
            pltpu.VMEM((HEADS, blk, qt), F32),
            pltpu.VMEM((HEADS, blk, qt), F32),
            pltpu.VMEM((HEADS, blk, qt), BF16),
            pltpu.VMEM((HEADS, blk, qt), BF16),
            pltpu.VMEM((2, 2 * n_z, rows, HW), F32),
            pltpu.VMEM((2, 2 * n_z, rows, HW), BF16),
            pltpu.VMEM((2 * n_z, rows, HW), BF16),
            pltpu.VMEM((n_z, rows, HW), BF16),
            pltpu.VMEM((n_z, rows, HW), BF16),
            pltpu.VMEM((n_z, rows, HW), F32),
            pltpu.VMEM((n_z, rows, HW), BF16),
            pltpu.VMEM((n_z, rows, HW), BF16),
            pltpu.VMEM((16, qt), F32),
            pltpu.VMEM((4, 2 * HEADS, qt), F32),
            pltpu.VMEM((n_z, 2 * HEADS, qt), F32),
            pltpu.VMEM((2, 16, qt), F32),
            pltpu.VMEM((n_clip, 2, HW), F32),
            dma((2, n_bank)),
            dma((2, n_z)),
            dma((2, n_z)),
            dma((2, 2 * n_z)),
            dma((2, max(4, n_z))),
            dma((2, max(4, n_z))),
            dma((2 + n_z,)),
            dma((2 + n_z,)),
            dma((n_clip,)),
            dma((n_clip,)),
        ],
        compiler_params=pltpu.CompilerParams(
            collective_id=0, has_side_effects=True, vmem_limit_bytes=56 * 1024 * 1024
        ),
    )(valid, q, keys[0], values[0], do, null_key.reshape(1, HW), null_value.reshape(1, HW))
    return gq[None, :own_rows], gk[None], gv[None], gnk[0], gnv[0]


def solution(mesh):
    return jax.shard_map(
        functools.partial(on_device, mesh.shape["clip"], mesh.shape["bank"]),
        mesh=mesh,
        in_specs=(
            P("clip", "bank", None),
            P("clip", "bank", None),
            P("clip", "bank", None),
            P("clip", "bank", None),
            P(),
            P(),
            P("clip"),
            P("clip", "bank"),
        ),
        out_specs=(
            P("clip", "bank", None),
            P("clip", "bank", None),
            P("clip", "bank", None),
            P(),
            P(),
        ),
        check_vma=False,
    )
```

time: 435 us -> 57.4 us (0.13)
  blocking collectives: 257 us -> 0 us
  local copies, waits for them, and re-layouts: 77.6 us -> 6.64 us
  matrix products: 47.8 us -> 0 us
  Pallas kernels: 0 us -> 47.2 us
  waiting for transfers between devices: 16.1 us -> 0 us
  other arithmetic: 15.8 us -> 1.24 us
  between operations: 15.6 us -> 1.96 us
    psum x3 -> x0, blocking collectives: 154 us -> none  [the longest x1 59.1 us: on_device(): row_delta = lax.psum(partial_delta, 'bank') + null_prob * null_dp]
    pmax x1 -> x0, blocking collectives: 57.8 us -> none  [on_device(): peaks_all = lax.pmax(local_peaks, 'bank')]
    dot_general x63 -> x0, matrix products: 47.8 us -> none  [the longest x24 21.5 us: block_scores(): jnp.dot(q_head, k_head.T, preferred_element_type=jnp.float32) * score_scale]
    pallas_call x0 -> x1, Pallas kernels: none -> 47.2 us  [on_device(): pl.pallas_call(functools.partial(kernel, n_clip, n_z, rows, blk), out_sha...]
    all_gather x2 -> x0, blocking collectives: 45.5 us -> none  [the longest x1 25.7 us: on_device(): lax.all_gather(queries[0], 'bank', axis=0, tiled=True)]
    dynamic_slice x72 -> x0, local copies, waits for them, and re-layouts: 41 us -> none  [the longest x48 24.1 us: on_device(): lax.map(third_pass, (probs_all, dprobs_all, q_heads, do_heads, row_delta))]
    dynamic_update_slice x72 -> x0, local copies, waits for them, and re-layouts: 27.3 us -> none  [the longest x36 16.8 us: on_device(): local_peaks, local_sums = lax.map(first_pass, (q_heads, k_heads))]
    reduce_scatter x1 -> x0, waiting for transfers between devices: 16.1 us -> none  [on_device(): lax.psum_scatter(product.reshape(row_count, HEADS * HD) * score_scale, 'b...]
  transfers between devices with their start and end apart: 1 -> 0, of which waited for: 1 -> 0; matrix products, arithmetic and copies ran while one was open for 1% -> 0% of each run, Pallas kernels for 0% -> 0%
where the time goes in v1:
time: 57.4 us; the launch traced here: 57 us
  Pallas kernels  47.2 us (82%)
  local copies, waits for them, and re-layouts  6.64 us (12%)
  between operations  1.96 us (3%)
  other arithmetic  1.24 us (2%)
    pallas_call x1, Pallas kernels, on_device(): pl.pallas_call(functools.partial(kernel, n_clip, n_z, rows, blk), out_sha...  47.2 us
    unnamed x11, local copies, waits for them, and re-layouts  4.75 us
    reshape x1, local copies, waits for them, and re-layouts, on_device(): null_key.reshape(1, HW)  1.29 us
    pallas_call x2, other arithmetic, on_device(): pl.pallas_call(functools.partial(kernel, n_clip, n_z, rows, blk), out_sha...  1.24 us

profile of v1, /device:TPU:0, one launch (start us, length us, event | category | flops | bytes accessed | tf_op | source)
XLA Modules:
  0.0 57.0 jit_solution(10064989887598134703)
XLA Ops:
  0.6 0.0 copy-start.3
  0.6 1.3 %reshape.16.nk_ref = bf16[1,1536]{1,0:T(2,128)(2,1)} reshape(bf16[1536]{0:T(1024)(128)(2,1)} %param.12) | data formatting | bytes 6144 | tf_op jit(solution)/shard_map/reshape | solution.py:323
  1.9 0.0 copy-done.3
  1.9 0.6 %reshape.17.nv_ref = bf16[1,1536]{1,0:T(2,128)(2,1)} reshape(bf16[1536]{0:T(1024)(128)(2,1)S(1)} %copy-done.3) | data formatting | bytes 6144 | tf_op jit(solution)/shard_map/reshape | solution.py:323
  3.8 47.2 %shard_map.119 = (bf16[16,1536]{1,0:T(8,128)(2,1)}, bf16[128,1536]{1,0:T(8,128)(2,1)}, bf16[128,1536]{1,0:T(8,128)(2,1)}, f32[1,1536]{1,0:T(1,128)}, f32[1,1536]{1,0:T(1,128)}) custom-call(s32[1,1]{1,0:T(1,128)S(6)} %min.6.valid_ref, bf16[16,1536]{1,0:T(8,128)(2,1)} %bitcast.13, bf16[128,1536]{1,0:T(8,128)(2,1)} %bitcast.9, bf16[128,1536]{1,0:T(8,128)(2,1)} %bitcast.10, ...), custom_call_target="tpu_custom_call" | custom-call | tf_op jit(solution)/shard_map/pallas_call | solution.py:278
  51.0 0.0 copy-start.2
  51.0 0.7 %copy-done.2 = f32[1,1536]{1,0:T(1,128)S(1)} copy-done((f32[1,1536]{1,0:T(1,128)S(1)}, f32[1,1536]{1,0:T(1,128)}, u32[]{:S(2)}) %copy-start.2) | copy-done | bytes 6168
  51.7 0.0 copy-start.1
  51.7 0.6 %reduce = f32[1536]{0:T(1024)} reduce(f32[1,1536]{1,0:T(1,128)S(1)} %copy-done.2, f32[]{:T(128)} %constant.13), dimensions={0}, to_apply=%get-tuple-element.13.reduce_sub_computation | reduce | bytes 12292 | tf_op jit(solution)/shard_map/pallas_call | solution.py:278
  52.3 0.1 copy-done.1
  52.4 0.6 %reduce.1 = f32[1536]{0:T(1024)} reduce(f32[1,1536]{1,0:T(1,128)S(1)} %copy-done.1, f32[]{:T(128)} %constant.13), dimensions={0}, to_apply=%get-tuple-element.14.reduce_sub_computation | reduce | bytes 12292 | tf_op jit(solution)/shard_map/pallas_call | solution.py:278
  53.0 1.4 %copy.18 = bf16[1,16,1536]{2,1,0:T(8,128)(2,1)} copy(bf16[1,16,1536]{2,1,0:T(8,128)(2,1)} %bitcast.15) | data formatting | bytes 98304
  54.5 0.0 copy-start
  54.5 1.8 %copy.19 = bf16[1,128,1536]{2,1,0:T(8,128)(2,1)} copy(bf16[1,128,1536]{2,1,0:T(8,128)(2,1)} %bitcast.12) | data formatting | bytes 786432
  56.3 0.0 copy-done
  56.3 0.7 %copy.20 = bf16[1,128,1536]{2,1,0:T(8,128)(2,1)} copy(bf16[1,128,1536]{2,1,0:T(8,128)(2,1)S(1)} %bitcast.11) | data formatting | bytes 786432
Async XLA Ops:
  0.6 1.3 %copy-start.3 = (bf16[1536]{0:T(1024)(128)(2,1)S(1)}, bf16[1536]{0:T(1024)(128)(2,1)}, u32[]{:S(2)}) copy-start(bf16[1536]{0:T(1024)(128)(2,1)} %param.13) | copy-start | bytes 9220
  51.0 0.7 %copy-start.2 = (f32[1,1536]{1,0:T(1,128)S(1)}, f32[1,1536]{1,0:T(1,128)}, u32[]{:S(2)}) copy-start(f32[1,1536]{1,0:T(1,128)} %get-tuple-element.13) | copy-start | bytes 18436
  51.7 0.7 %copy-start.1 = (f32[1,1536]{1,0:T(1,128)S(1)}, f32[1,1536]{1,0:T(1,128)}, u32[]{:S(2)}) copy-start(f32[1,1536]{1,0:T(1,128)} %get-tuple-element.14) | copy-start | bytes 18436
  54.5 1.8 %copy-start = (bf16[128,1536]{1,0:T(8,128)(2,1)S(1)}, bf16[128,1536]{1,0:T(8,128)(2,1)}, u32[]{:S(2)}) copy-start(bf16[128,1536]{1,0:T(8,128)(2,1)} %get-tuple-element.12) | copy-start | bytes 1179652
